TPU v7x, 256 devices: a whole 4x4x8 slice. The times are simulated.
256 devices in a mesh: dp: 32 (over z, y_hi, core), ctx: 8 (over x, y_lo).
Axes of the slice: x: 4, y: 4 (y_hi: 2, y_lo: 2; y = y_hi * 2 + y_lo), z: 8, core: 2. Of those that a mesh axis runs over, the one named last changes fastest.
Arguments:
- q_heads: bfloat16 [32, 1536, 2048], P('dp', 'ctx'), may hold values from -8 to 8
- keys: bfloat16 [32, 1536, 128], P('dp', 'ctx'), may hold values from -8 to 8
- values: bfloat16 [32, 1536, 128], P('dp', 'ctx'), may hold values from -6 to 6
- out_grad: bfloat16 [32, 1536, 2048], P('dp', 'ctx'), may hold values from -0.29882812 to 0.29882812
- hidden_in: bfloat16 [32, 1536, 16384], P('dp', 'ctx'), may hold values from -6 to 6
- doc_lengths: int32 [32, 8], P('dp'), may hold values from 1 to 576, 1536 in all within a row
- span_order: int32 [16], replicated, may hold values from 0 to 15, each once
- m_codes: int32 [16384, 256], P('dp'), may hold values from -127 to 127
- m_scales: float32 [2048], P('dp'), may hold values from 0.05 to 0.5
- v_codes: int32 [16384, 256], P('dp'), may hold values from 1 to 255
- v_scales: float32 [2048], P('dp'), may hold values from 0.05 to 1
Outputs:
- dq: bfloat16 [32, 1536, 2048], P('dp', 'ctx')
- update: float32 [16384, 256], P('dp')
- m_norm: float32 [16384, 256], P('dp')
- m_absmax: float32 [2048], P('dp')
- v_norm: float32 [16384, 256], P('dp')
- v_absmax: float32 [2048], P('dp')
Inputs may be any that keep to these rules, and one draw needn't show every extreme that they name: `doc_lengths`: each sequence's 8 lengths sum to 1536. `span_order`: each stored block names a different position block.
All inputs are finite; a program needn't handle non-finite values. Where the computation divides by a largest or mean magnitude, that divisor is 1e-20 or more.
Results may differ from a plain program's by a relative error of at most 0.0078.
Values may be sent and summed in bfloat16 or wider, within the bound.
A program may use at most 128 MiB of HBM per device.

v0:
```python
import math
import jax
import jax.numpy as jnp
from jax import lax
from jax.sharding import PartitionSpec as P

BLOCK = 2048
STEP = 10


def positions(order, span, total):
    rows = jnp.arange(total, dtype=jnp.int32)
    slot = rows // span
    match = slot[:, None] == jnp.arange(order.shape[0], dtype=jnp.int32)[None, :]
    first = jnp.sum(jnp.where(match, order[None, :], 0), axis=1)
    return first * span + rows % span


def documents(pos, lengths):
    ends = jnp.cumsum(lengths)
    return jnp.sum((pos[:, None] >= ends[None, :]).astype(jnp.int32), axis=1)


def adam_blocks(grad, m_codes, m_scales, v_codes, v_scales):
    shape = grad.shape
    g_blocks = grad.reshape(-1, BLOCK)
    m_old = m_codes.reshape(-1, BLOCK).astype(jnp.float32) / 127.0 * m_scales[:, None]
    v_old = v_codes.reshape(-1, BLOCK).astype(jnp.float32) / 255.0 * v_scales[:, None]
    moment = 0.9 * m_old + 0.1 * g_blocks
    second = 0.95 * v_old + 0.05 * g_blocks * g_blocks
    update = moment / (1.0 - 0.9**STEP) / (jnp.sqrt(second / (1.0 - 0.95**STEP)) + 1e-08)
    m_absmax = jnp.max(jnp.abs(moment), axis=1)
    v_absmax = jnp.max(second, axis=1)
    m_norm = moment / (m_absmax[:, None] + 1e-06)
    v_norm = second / (v_absmax[:, None] + 1e-06)
    return (update.reshape(shape), m_norm.reshape(shape), m_absmax, v_norm.reshape(shape), v_absmax)


def contract_rows(left, right):
    return lax.dot_general(
        left, right, (((0,), (0,)), ((), ())), preferred_element_type=jnp.float32
    )


def contract_cols(left, right):
    return lax.dot_general(
        left, right, (((1,), (1,)), ((), ())), preferred_element_type=jnp.float32
    )


def shards(
    q_heads,
    keys,
    values,
    out_grad,
    hidden_in,
    doc_lengths,
    span_order,
    m_codes,
    m_scales,
    v_codes,
    v_scales,
):
    rows = q_heads.shape[1]
    head_dim = keys.shape[2]
    heads_width = q_heads.shape[2]
    nheads = heads_width // head_dim
    scale = 1.0 / math.sqrt(head_dim)
    total = rows * lax.axis_size("ctx")
    key_all, value_all = (
        lax.all_gather(keys[0], "ctx", axis=0, tiled=True),
        lax.all_gather(values[0], "ctx", axis=0, tiled=True),
    )
    pos = positions(span_order, rows // 2, total)
    doc = documents(pos, doc_lengths[0])
    first_row = lax.axis_index("ctx") * rows
    query_pos = lax.dynamic_slice_in_dim(pos, first_row, rows)
    query_doc = lax.dynamic_slice_in_dim(doc, first_row, rows)
    queries = q_heads[0].reshape(rows * nheads, head_dim)
    grads_out = out_grad[0].reshape(rows * nheads, head_dim)
    width = min(512, total)
    nblocks = total // width
    blocks = (
        key_all.reshape(nblocks, width, head_dim),
        value_all.reshape(nblocks, width, head_dim),
        pos.reshape(nblocks, width),
        doc.reshape(nblocks, width),
    )

    def block_masks(key_pos, key_doc):
        small = (key_pos[None, :] <= query_pos[:, None]) & (key_doc[None, :] == query_doc[:, None])
        wide = jnp.broadcast_to(small[:, None, :], (rows, nheads, width)).reshape(
            rows * nheads, width
        )
        return (small, wide)

    def forward_terms(carry, block):
        key_block, value_block, key_pos, key_doc = block
        small, wide = block_masks(key_pos, key_doc)
        top, denom, weighted = carry
        scores = contract_cols(queries, key_block) * scale
        dprob = contract_cols(grads_out, value_block)
        new_top = jnp.maximum(top, jnp.max(jnp.where(wide, scores, -1e30), axis=1, keepdims=True))
        expo = jnp.where(wide, jnp.exp(scores - new_top), 0.0)
        factor = jnp.exp(top - new_top)
        result = (
            new_top,
            denom * factor + jnp.sum(expo, axis=1, keepdims=True),
            weighted * factor + jnp.sum(expo * dprob, axis=1, keepdims=True),
        )
        return (result, None)

    column = jnp.zeros((rows * nheads, 1), jnp.float32)
    start_state = (column - 1e30, column, column)
    (top, denom, weighted), unused = lax.scan(forward_terms, start_state, blocks)
    delta = weighted / denom

    def backward_terms(accum, block):
        key_block, value_block, key_pos, key_doc = block
        small, wide = block_masks(key_pos, key_doc)
        acc = accum
        scores = contract_cols(queries, key_block) * scale
        dprob = contract_cols(grads_out, value_block)
        prob = jnp.where(wide, jnp.exp(scores - top), 0.0) / denom
        prob_low = prob.astype(jnp.bfloat16)
        dscore = (prob * (dprob - delta)).astype(jnp.bfloat16)
        acc = acc + jnp.dot(dscore, key_block, preferred_element_type=jnp.float32)
        dkey = contract_rows(dscore, queries) * scale
        dvalue = contract_rows(prob_low, grads_out)
        return (acc, jnp.concatenate([dkey, dvalue], axis=1))

    dq_sum, pieces = lax.scan(
        backward_terms, jnp.zeros((rows * nheads, head_dim), jnp.float32), blocks
    )
    dq = (dq_sum * scale).reshape(1, rows, heads_width).astype(jnp.bfloat16)
    partial_grads = pieces.reshape(total, 2 * head_dim)
    own = lax.psum_scatter(partial_grads, "ctx", scatter_dimension=0, tiled=True)
    own_low = own.astype(jnp.bfloat16)
    layer_in = hidden_in[0]
    grad = lax.psum_scatter(contract_rows(layer_in, own_low), "dp", scatter_dimension=0, tiled=True)
    grad = lax.psum(grad, "ctx")
    update, m_norm, m_absmax, v_norm, v_absmax = adam_blocks(
        grad, m_codes, m_scales, v_codes, v_scales
    )
    return (dq, update, m_norm, m_absmax, v_norm, v_absmax)


def solution(mesh):
    in_specs = (
        P("dp", "ctx", None),
        P("dp", "ctx", None),
        P("dp", "ctx", None),
        P("dp", "ctx", None),
        P("dp", "ctx", None),
        P("dp", None),
        P(),
        P("dp", None),
        P("dp"),
        P("dp", None),
        P("dp"),
    )
    out_specs = (
        P("dp", "ctx", None),
        P("dp", None),
        P("dp", None),
        P("dp"),
        P("dp", None),
        P("dp"),
    )
    return jax.shard_map(shards, mesh=mesh, in_specs=in_specs, out_specs=out_specs, check_vma=False)
```

profile of v0, /device:TPU:32, one launch (start us, length us, event | category | flops | bytes accessed | tf_op | source)
XLA Modules:
  0.0 549.1 jit_solution(15692817767166467675)
XLA Ops:
  7.3 0.8 select_reduce_fusion
  8.1 0.8 reduce-window.8
  11.0 29.1 %all-gather = bf16[1,1536,128]{2,1,0:T(8,128)(2,1)S(1)} all-gather(bf16[1,192,128]{2,1,0:T(8,128)(2,1)} %param.16), channel_id=2, replica_groups=mesh['dp'=32,'ctx'=8] {'ctx'}, dimensions={1}, use_global_device_ids=true | all-gather | bytes 442368 | tf_op jit(solution)/shard_map/all_gather | solution.py:71
  40.1 1.4 reshape_squeeze.6
  41.5 30.8 %all-gather.1 = bf16[1,1536,128]{2,1,0:T(8,128)(2,1)} all-gather(bf16[1,192,128]{2,1,0:T(8,128)(2,1)} %param.17), channel_id=3, replica_groups=mesh['dp'=32,'ctx'=8] {'ctx'}, dimensions={1}, use_global_device_ids=true | all-gather | bytes 442368 | tf_op jit(solution)/shard_map/all_gather | solution.py:72
  72.7 46.8 %while.28 = (s32[]{:T(128)}, f32[3072,1]{0,1:T(1,128)}, f32[3072,1]{0,1:T(1,128)}, f32[3072,1]{0,1:T(1,128)}, s32[3,512]{1,0:T(4,128)}, /*index=5*/s32[192]{0:T(...) while((s32[]{:T(128)}, f32[3072,1]{0,1:T(1,128)}, ...), condition=%wide.region_7.8_spmd.clone, body=%wide.region_3.7_spmd.clone.sunk | while | flops 824497152 | bytes 55990092 | solution.py:115
  72.7 0.7 constant_dynamic-slice_fusion.6
  73.5 0.8 compare_and_fusion.4
  74.7 1.7 copy.45
  76.4 3.9 fusion.79
  80.3 5.2 fusion.81
  85.5 1.6 fusion.82
  87.9 0.7 constant_dynamic-slice_fusion.6
  88.6 0.8 compare_and_fusion.4
  89.8 1.7 copy.45
  91.5 3.9 fusion.79
  95.4 0.7 fusion.80
  96.1 5.2 fusion.81
  101.3 1.6 fusion.82
  104.4 0.8 compare_and_fusion.4
  105.6 1.7 copy.45
  107.3 3.8 fusion.79
  111.2 0.7 fusion.80
  111.9 5.2 fusion.81
  117.1 1.6 fusion.82
  119.5 1.3 div.70
  120.9 55.8 %while.29 = (s32[]{:T(128)}, f32[3072,128]{1,0:T(8,128)}, f32[3,512,256]{2,1,0:T(8,128)}, s32[3,512]{1,0:T(4,128)}, s32[192]{0:T(256)S(1)}, /*index=5*/s32[3,512...) while((s32[]{:T(128)}, f32[3072,128]{1,0:T(8,128)}, ...), condition=%wide.region_9.10_spmd.clone, body=%wide.region_8.9_spmd.clone.sunk | while | flops 2027126784 | bytes 108267456 | solution.py:132
  120.9 0.9 constant_dynamic-slice_fusion.7
  121.7 0.8 compare_and_fusion.5
  123.0 1.7 copy.46
  124.7 1.9 fusion.94
  126.7 2.9 fusion.95
  129.7 2.2 convolution_add_fusion.2
  131.9 1.1 copy-done.2
  133.0 2.3 fusion.96
  135.3 2.3 convolution_multiply_fusion.2
  137.9 0.8 constant_dynamic-update-slice_fusion.2
  139.2 0.9 constant_dynamic-slice_fusion.7
  140.1 0.8 compare_and_fusion.5
  141.3 1.7 copy.46
  143.0 1.9 fusion.94
  145.0 2.9 fusion.95
  148.0 3.8 convolution_add_fusion.2
  151.7 2.3 fusion.96
  154.1 2.3 convolution_multiply_fusion.2
  156.6 0.8 constant_dynamic-update-slice_fusion.2
  157.9 0.9 constant_dynamic-slice_fusion.7
  158.8 0.8 compare_and_fusion.5
  160.0 1.7 copy.46
  161.8 1.9 fusion.94
  163.7 2.9 fusion.95
  166.7 3.8 convolution_add_fusion.2
  170.5 2.3 fusion.96
  172.8 2.3 convolution_multiply_fusion.2
  175.4 0.8 constant_dynamic-update-slice_fusion.2
  176.7 49.4 %reduce-scatter.3.cloned.1.call-done = f32[192,256]{1,0:T(8,128)} async-done(((f32[1536,256]{1,0:T(8,128)}), f32[192,256]{1,0:T(8,128)}) %reduce-scatter.3.cloned.1.call-update) | async-done | bytes 196624 | tf_op jit(solution)/shard_map/reduce_scatter | solution.py:137
  226.2 11.0 %convolution_bitcast_fusion = f32[16384,256]{0,1:T(8,128)} fusion(bf16[1,192,16384]{2,1,0:T(8,128)(2,1)} %param.19, f32[192,256]{1,0:T(8,128)} %reduce-scatter.3.cloned.1.call-done), kind=kOutput, calls=%fused_computation.49 | convolution fusion | flops 1610661888 | bytes 23265280 | tf_op jit(solution)/shard_map/dot_general | solution.py:40
  237.3 218.4 %reduce-scatter.5.cloned.1.call-done = f32[512,256]{0,1:T(8,128)} async-done(((f32[16384,256]{0,1:T(8,128)}), f32[512,256]{0,1:T(8,128)}) %reduce-scatter.5.cloned.1.call-update) | async-done | bytes 524304 | tf_op jit(solution)/shard_map/reduce_scatter | solution.py:140
  455.9 1.2 convert_element_type.40
  457.9 79.3 %all-reduce.2.cloned.1.call-done = f32[512,256]{0,1:T(8,128)} async-done(((f32[512,256]{0,1:T(8,128)}), f32[512,256]{0,1:T(8,128)}) %all-reduce.2.cloned.1.call-update) | async-done | bytes 524304 | tf_op jit(solution)/shard_map/psum | solution.py:141
  537.2 1.3 abs_reduce_fusion
  539.6 1.0 copy.37
  540.6 1.0 copy.38
  541.6 1.0 copy.39
  (165 shorter events, 12.0 us)
Async XLA Ops:
  7.2 65.2 %copy-start.10 = (bf16[1,192,2048]{2,1,0:T(8,128)(2,1)S(1)}, bf16[1,192,2048]{2,1,0:T(8,128)(2,1)}, u32[]{:S(2)}) copy-start(bf16[1,192,2048]{2,1,0:T(8,128)(2,1)} %param.18) | copy-start | bytes 2359300
  7.2 219.0 %reduce-scatter.3.cloned.1.call-start = ((), (), s32[]{:S(2)}) async-start(), calls=%async_computation.2 | async-start | bytes 1769472 | tf_op jit(solution)/shard_map/reduce_scatter | solution.py:137
  80.3 5.2 copy-start
  85.4 1.7 copy-start.8
  85.5 1.7 copy-start.14
  85.5 1.7 copy-start.17
  87.2 0.6 copy-start.15
  87.2 0.6 copy-start.18
  96.1 5.2 copy-start
  101.3 1.7 copy-start.8
  101.3 1.7 copy-start.14
  101.3 1.7 copy-start.17
  103.1 0.6 copy-start.15
  103.1 0.6 copy-start.18
  111.9 5.2 copy-start
  117.1 1.7 copy-start.8
  117.1 1.7 copy-start.14
  117.1 1.7 copy-start.17
  118.9 0.6 copy-start.15
  118.9 0.6 copy-start.18
  120.9 5.8 %copy-start.4 = (bf16[3072,128]{1,0:T(8,128)(2,1)}, bf16[3072,128]{1,0:T(8,128)(2,1)S(1)}, u32[]{:S(2)}) copy-start(bf16[3072,128]{1,0:T(8,128)(2,1)S(1)} %get-tuple-element.577) | copy-start | bytes 2359300 | tf_op jit(solution)/shard_map/while
  120.9 5.8 %copy-start.6 = (bf16[3072,128]{1,0:T(8,128)(2,1)}, bf16[3072,128]{1,0:T(8,128)(2,1)S(1)}, u32[]{:S(2)}) copy-start(bf16[3072,128]{1,0:T(8,128)(2,1)S(1)} %get-tuple-element.581) | copy-start | bytes 2359300 | tf_op jit(solution)/shard_map/while
  120.9 3.8 copy-start.9
  120.9 3.8 copy-start.16
  124.7 2.0 copy-start.13
  126.7 3.0 copy-start.1
  129.7 3.4 copy-start.2
  137.6 1.1 copy-start.5
  137.6 1.6 copy-start.7
  139.2 5.8 %copy-start.4 = (bf16[3072,128]{1,0:T(8,128)(2,1)}, bf16[3072,128]{1,0:T(8,128)(2,1)S(1)}, u32[]{:S(2)}) copy-start(bf16[3072,128]{1,0:T(8,128)(2,1)S(1)} %get-tuple-element.577) | copy-start | bytes 2359300 | tf_op jit(solution)/shard_map/while
  139.2 5.8 %copy-start.6 = (bf16[3072,128]{1,0:T(8,128)(2,1)}, bf16[3072,128]{1,0:T(8,128)(2,1)S(1)}, u32[]{:S(2)}) copy-start(bf16[3072,128]{1,0:T(8,128)(2,1)S(1)} %get-tuple-element.581) | copy-start | bytes 2359300 | tf_op jit(solution)/shard_map/while
  139.2 3.8 copy-start.9
  139.2 3.8 copy-start.16
  143.0 2.0 copy-start.13
  145.0 3.0 copy-start.1
  148.0 3.8 copy-start.2
  156.4 1.1 copy-start.5
  156.4 1.6 copy-start.7
  157.9 5.8 %copy-start.4 = (bf16[3072,128]{1,0:T(8,128)(2,1)}, bf16[3072,128]{1,0:T(8,128)(2,1)S(1)}, u32[]{:S(2)}) copy-start(bf16[3072,128]{1,0:T(8,128)(2,1)S(1)} %get-tuple-element.577) | copy-start | bytes 2359300 | tf_op jit(solution)/shard_map/while
  157.9 5.8 %copy-start.6 = (bf16[3072,128]{1,0:T(8,128)(2,1)}, bf16[3072,128]{1,0:T(8,128)(2,1)S(1)}, u32[]{:S(2)}) copy-start(bf16[3072,128]{1,0:T(8,128)(2,1)S(1)} %get-tuple-element.581) | copy-start | bytes 2359300 | tf_op jit(solution)/shard_map/while
  157.9 3.8 copy-start.9
  157.9 3.8 copy-start.16
  161.7 2.0 copy-start.13
  163.7 3.0 copy-start.1
  166.7 3.8 copy-start.2
  175.1 1.1 copy-start.5
  175.1 1.6 copy-start.7
  176.7 279.0 %reduce-scatter.5.cloned.1.call-start = ((), (), s32[]{:S(2)}) async-start(), calls=%async_computation.3 | async-start | bytes 17301504 | tf_op jit(solution)/shard_map/reduce_scatter | solution.py:140
  237.2 218.6 %copy-start.3 = (f32[3072,128]{1,0:T(8,128)S(1)}, f32[3072,128]{1,0:T(8,128)}, u32[]{:S(2)}) copy-start(f32[3072,128]{1,0:T(8,128)} %get-tuple-element.146) | copy-start | bytes 4718596
  237.2 219.9 %copy-start.21 = (f32[64]{0:T(128)S(1)}, f32[64]{0:T(128)}, u32[]{:S(2)}) copy-start(f32[64]{0:T(128)} %param.23) | copy-start | bytes 772
  237.2 220.1 %copy-start.11 = (s32[512,256]{1,0:T(8,128)S(1)}, s32[512,256]{1,0:T(8,128)}, u32[]{:S(2)}) copy-start(s32[512,256]{1,0:T(8,128)} %param.22) | copy-start | bytes 1572868
  237.2 220.3 %copy-start.22 = (f32[64]{0:T(128)S(1)}, f32[64]{0:T(128)}, u32[]{:S(2)}) copy-start(f32[64]{0:T(128)} %param.25) | copy-start | bytes 772
  237.2 220.4 %copy-start.12 = (s32[512,256]{1,0:T(8,128)S(1)}, s32[512,256]{1,0:T(8,128)}, u32[]{:S(2)}) copy-start(s32[512,256]{1,0:T(8,128)} %param.24) | copy-start | bytes 1572868
  237.2 300.0 %all-reduce.2.cloned.1.call-start = ((), (), s32[]{:S(2)}) async-start(), calls=%async_computation.4 | async-start | bytes 1048576 | tf_op jit(solution)/shard_map/psum | solution.py:141
  538.7 3.9 copy-start.19
  539.1 3.5 copy-start.20
Sparse Core Ops, SparseCore 0:
  176.8 49.3 reduce-scatter.2
  237.3 218.3 reduce-scatter.4
  458.5 78.6 all-reduce.1
where the time goes:
time: 550 us; the launch traced here: 549 us
  waiting for transfers between devices  347 us (63%)
  matrix products  76.2 us (14%)
  blocking collectives  59.9 us (11%)
  local copies, waits for them, and re-layouts  33.6 us (6%)
  other arithmetic  17.2 us (3%)
  between operations  14 us (3%)
    reduce_scatter x1, waiting for transfers between devices, shards(): lax.psum_scatter(contract_rows(layer_in, own_low), 'dp', scatter_dimensio...  218 us
    psum x1, waiting for transfers between devices, shards(): grad = lax.psum(grad, 'ctx')  79.3 us
    reduce_scatter x1, waiting for transfers between devices, shards(): lax.psum_scatter(partial_grads, 'ctx', scatter_dimension=0, tiled=True)  49.4 us
    dot_general x12, matrix products, contract_cols(): lax.dot_general(left, right, (((1,), (1,)), ((), ())), preferred_element_...  41.6 us
    all_gather x1, blocking collectives, shards(): lax.all_gather(values[0], 'ctx', axis=0, tiled=True)  30.8 us
    all_gather x1, blocking collectives, shards(): lax.all_gather(keys[0], 'ctx', axis=0, tiled=True)  29.1 us
    dot_general x7, matrix products, contract_rows(): lax.dot_general(left, right, (((0,), (0,)), ((), ())), preferred_element_...  24.8 us
  transfers between devices with their start and end apart: 3, of which 3 were waited for; matrix products, arithmetic and copies ran while one was open for 0% of the time, Pallas kernels for 0%

commit v1 on v0

--- a/solution.py
+++ b/solution.py
@@ -61,6 +61,15 @@
     v_codes,
     v_scales,
 ):
+
+    def use_values(m, array_dim):
+        built = jax.lax.axis_size("ctx")
+        big = jnp.stack([m] * built)
+        field_out = jnp.concatenate(
+            jax.lax.all_to_all(big, axis_name="ctx", split_axis=0, concat_axis=0), axis=array_dim
+        )
+        return field_out
+
     rows = q_heads.shape[1]
     head_dim = keys.shape[2]
     heads_width = q_heads.shape[2]
@@ -69,7 +78,7 @@
     total = rows * lax.axis_size("ctx")
     key_all, value_all = (
         lax.all_gather(keys[0], "ctx", axis=0, tiled=True),
-        lax.all_gather(values[0], "ctx", axis=0, tiled=True),
+        use_values(values[0], 0),
     )
     pos = positions(span_order, rows // 2, total)
     doc = documents(pos, doc_lengths[0])

time: 550 us -> 526 us (0.956)
  blocking collectives: 59.9 us -> 29.2 us
    all_gather x1 -> x0, blocking collectives: 30.8 us -> none  [shards(): lax.all_gather(values[0], 'ctx', axis=0, tiled=True)]
  transfers between devices with their start and end apart: 3 -> 4, of which waited for: 3 -> 3; matrix products, arithmetic and copies ran while one was open for 0% -> 2% of each run, Pallas kernels for 0% -> 0%
where the time goes in v1:
time: 526 us; the launch traced here: 525 us
  waiting for transfers between devices  345 us (66%)
  matrix products  75.8 us (14%)
  local copies, waits for them, and re-layouts  37 us (7%)
  blocking collectives  29.2 us (6%)
  other arithmetic  16.9 us (3%)
  between operations  14 us (3%)
  starting transfers between devices  5.43 us (1%)
    reduce_scatter x1, waiting for transfers between devices, shards(): lax.psum_scatter(contract_rows(layer_in, own_low), 'dp', scatter_dimensio...  216 us
    psum x1, waiting for transfers between devices, shards(): grad = lax.psum(grad, 'ctx')  80.1 us
    reduce_scatter x1, waiting for transfers between devices, shards(): lax.psum_scatter(partial_grads, 'ctx', scatter_dimension=0, tiled=True)  49.2 us
    dot_general x12, matrix products, contract_cols(): lax.dot_general(left, right, (((1,), (1,)), ((), ())), preferred_element_...  41.2 us
    all_gather x1, blocking collectives, shards(): lax.all_gather(keys[0], 'ctx', axis=0, tiled=True)  29.2 us
    dot_general x7, matrix products, contract_rows(): lax.dot_general(left, right, (((0,), (0,)), ((), ())), preferred_element_...  24.8 us
  transfers between devices with their start and end apart: 4, of which 3 were waited for; matrix products, arithmetic and copies ran while one was open for 2% of the time, Pallas kernels for 0%

profile of v1, /device:TPU:32, one launch (start us, length us, event | category | flops | bytes accessed | tf_op | source)
XLA Modules:
  0.0 524.6 jit_solution(7572806509579815984)
XLA Ops:
  7.2 1.7 stack.3
  8.9 5.3 %all-to-all-start = ((bf16[8,192,128]{2,1,0:T(8,128)(2,1)}), bf16[8,192,128]{2,1,0:T(8,128)(2,1)}, u32[]{:S(2)}, u32[]{:S(2)}) async-start(bf16[8,192,128]{2,1,0:T(8,128)(2,1)} %stack.3), calls=%async_computation | async-start | bytes 786432 | tf_op jit(solution)/shard_map/all_to_all | solution.py:69
  14.2 0.7 select_reduce_fusion
  15.0 0.8 reduce-window.8
  17.2 1.4 reshape_squeeze.6
  19.1 29.2 %all-gather = bf16[1,1536,128]{2,1,0:T(8,128)(2,1)S(1)} all-gather(bf16[1,192,128]{2,1,0:T(8,128)(2,1)S(1)} %copy-done.17), channel_id=2, replica_groups=mesh['dp'=32,'ctx'=8] {'ctx'}, dimensions={1}, use_global_device_ids=true | all-gather | bytes 442368 | tf_op jit(solution)/shard_map/all_gather | solution.py:80
  48.9 46.7 %while.28 = (s32[]{:T(128)}, f32[3072,1]{0,1:T(1,128)}, f32[3072,1]{0,1:T(1,128)}, f32[3072,1]{0,1:T(1,128)}, s32[3,512]{1,0:T(4,128)}, /*index=5*/s32[192]{0:T(...) while((s32[]{:T(128)}, f32[3072,1]{0,1:T(1,128)}, ...), condition=%wide.region_7.8_spmd.clone, body=%wide.region_3.7_spmd.clone.sunk | while | flops 824497152 | bytes 55990092 | solution.py:124
  49.6 0.8 compare_and_fusion.4
  50.8 1.7 copy.45
  52.5 3.8 fusion.79
  56.4 5.2 fusion.81
  61.6 1.6 fusion.82
  64.7 0.8 compare_and_fusion.4
  65.9 1.7 copy.45
  67.6 3.8 fusion.79
  71.4 0.7 fusion.80
  72.2 5.2 fusion.81
  77.4 1.6 fusion.82
  80.5 0.8 compare_and_fusion.4
  81.7 1.7 copy.45
  83.4 3.8 fusion.79
  87.2 0.7 fusion.80
  88.0 5.2 fusion.81
  93.2 1.6 fusion.82
  95.6 1.3 div.70
  96.9 55.2 %while.29 = (s32[]{:T(128)}, f32[3072,128]{1,0:T(8,128)}, f32[3,512,256]{2,1,0:T(8,128)}, s32[3,512]{1,0:T(4,128)}, s32[192]{0:T(256)S(1)}, /*index=5*/s32[3,512...) while((s32[]{:T(128)}, f32[3072,128]{1,0:T(8,128)}, ...), condition=%wide.region_9.10_spmd.clone, body=%wide.region_8.9_spmd.clone.sunk | while | flops 2027126784 | bytes 108218272 | solution.py:141
  96.9 0.9 constant_dynamic-slice_fusion.7
  97.8 0.8 compare_and_fusion.5
  99.0 1.7 copy.46
  100.7 1.9 fusion.94
  102.7 2.8 fusion.95
  105.5 2.2 convolution_add_fusion.2
  107.7 1.1 copy-done.2
  108.9 2.3 fusion.96
  111.2 2.3 convolution_multiply_fusion.2
  113.8 0.8 constant_dynamic-update-slice_fusion.2
  115.1 0.9 constant_dynamic-slice_fusion.7
  115.9 0.8 compare_and_fusion.5
  117.1 1.7 copy.46
  118.8 1.9 fusion.94
  120.8 2.8 fusion.95
  123.6 3.8 convolution_add_fusion.2
  127.4 2.3 fusion.96
  129.7 2.3 convolution_multiply_fusion.2
  132.3 0.8 constant_dynamic-update-slice_fusion.2
  133.6 0.9 constant_dynamic-slice_fusion.7
  134.5 0.8 compare_and_fusion.5
  135.7 1.7 copy.46
  137.4 1.9 fusion.94
  139.4 2.8 fusion.95
  142.2 3.8 convolution_add_fusion.2
  146.0 2.3 fusion.96
  148.3 2.3 convolution_multiply_fusion.2
  150.9 0.8 constant_dynamic-update-slice_fusion.2
  152.2 49.2 %reduce-scatter.3.cloned.1.call-done = f32[192,256]{1,0:T(8,128)} async-done(((f32[1536,256]{1,0:T(8,128)}), f32[192,256]{1,0:T(8,128)}) %reduce-scatter.3.cloned.1.call-update) | async-done | bytes 196624 | tf_op jit(solution)/shard_map/reduce_scatter | solution.py:146
  201.4 11.0 %convolution_bitcast_fusion = f32[16384,256]{0,1:T(8,128)} fusion(bf16[1,192,16384]{2,1,0:T(8,128)(2,1)} %param.19, f32[192,256]{1,0:T(8,128)} %reduce-scatter.3.cloned.1.call-done), kind=kOutput, calls=%fused_computation.49 | convolution fusion | flops 1610661888 | bytes 23265280 | tf_op jit(solution)/shard_map/dot_general | solution.py:40
  213.9 1.2 copy.36
  215.1 216.1 %reduce-scatter.5.cloned.1.call-done = f32[512,256]{0,1:T(8,128)} async-done(((f32[16384,256]{0,1:T(8,128)}), f32[512,256]{0,1:T(8,128)}) %reduce-scatter.5.cloned.1.call-update) | async-done | bytes 524304 | tf_op jit(solution)/shard_map/reduce_scatter | solution.py:149
  431.4 1.2 convert_element_type.40
  432.6 80.1 %all-reduce.2.cloned.1.call-done = f32[512,256]{0,1:T(8,128)} async-done(((f32[512,256]{0,1:T(8,128)}), f32[512,256]{0,1:T(8,128)}) %all-reduce.2.cloned.1.call-update) | async-done | bytes 524304 | tf_op jit(solution)/shard_map/psum | solution.py:150
  512.7 1.3 abs_reduce_fusion
  515.1 1.0 copy.37
  516.1 1.0 copy.38
  517.1 1.0 copy.39
  (161 shorter events, 14.0 us)
Async XLA Ops:
  7.2 11.5 %copy-start.10 = (bf16[1,192,2048]{2,1,0:T(8,128)(2,1)S(1)}, bf16[1,192,2048]{2,1,0:T(8,128)(2,1)}, u32[]{:S(2)}) copy-start(bf16[1,192,2048]{2,1,0:T(8,128)(2,1)} %param.18) | copy-start | bytes 2359300
  7.2 11.9 %copy-start.17 = (bf16[1,192,128]{2,1,0:T(8,128)(2,1)S(1)}, bf16[1,192,128]{2,1,0:T(8,128)(2,1)}, u32[]{:S(2)}) copy-start(bf16[1,192,128]{2,1,0:T(8,128)(2,1)} %param.16) | copy-start | bytes 147460
  8.9 40.0 %all-to-all-start = ((bf16[8,192,128]{2,1,0:T(8,128)(2,1)}), bf16[8,192,128]{2,1,0:T(8,128)(2,1)}, u32[]{:S(2)}, u32[]{:S(2)}) async-start(bf16[8,192,128]{2,1,0:T(8,128)(2,1)} %stack.3), calls=%async_computation | async-start | bytes 786432 | tf_op jit(solution)/shard_map/all_to_all | solution.py:69
  14.2 187.2 %reduce-scatter.3.cloned.1.call-start = ((), (), s32[]{:S(2)}) async-start(), calls=%async_computation.3 | async-start | bytes 1769472 | tf_op jit(solution)/shard_map/reduce_scatter | solution.py:146
  56.4 5.2 copy-start
  61.6 1.7 copy-start.8
  61.6 1.7 copy-start.12
  61.6 1.7 copy-start.15
  63.3 0.6 copy-start.13
  63.4 0.6 copy-start.16
  72.2 5.2 copy-start
  77.4 1.7 copy-start.8
  77.4 1.7 copy-start.12
  77.4 1.7 copy-start.15
  79.1 0.6 copy-start.13
  79.2 0.6 copy-start.16
  88.0 5.2 copy-start
  93.1 1.7 copy-start.8
  93.2 1.7 copy-start.12
  93.2 1.7 copy-start.15
  94.9 0.6 copy-start.13
  94.9 0.6 copy-start.16
  96.9 5.7 %copy-start.4 = (bf16[3072,128]{1,0:T(8,128)(2,1)}, bf16[3072,128]{1,0:T(8,128)(2,1)S(1)}, u32[]{:S(2)}) copy-start(bf16[3072,128]{1,0:T(8,128)(2,1)S(1)} %get-tuple-element.577) | copy-start | bytes 2359300 | tf_op jit(solution)/shard_map/while
  96.9 5.7 %copy-start.6 = (bf16[3072,128]{1,0:T(8,128)(2,1)}, bf16[3072,128]{1,0:T(8,128)(2,1)S(1)}, u32[]{:S(2)}) copy-start(bf16[3072,128]{1,0:T(8,128)(2,1)S(1)} %get-tuple-element.581) | copy-start | bytes 2359300 | tf_op jit(solution)/shard_map/while
  96.9 3.8 copy-start.9
  96.9 3.8 copy-start.14
  102.7 2.8 copy-start.1
  105.5 3.4 copy-start.2
  113.5 1.1 copy-start.5
  113.5 1.6 copy-start.7
  115.0 5.7 %copy-start.4 = (bf16[3072,128]{1,0:T(8,128)(2,1)}, bf16[3072,128]{1,0:T(8,128)(2,1)S(1)}, u32[]{:S(2)}) copy-start(bf16[3072,128]{1,0:T(8,128)(2,1)S(1)} %get-tuple-element.577) | copy-start | bytes 2359300 | tf_op jit(solution)/shard_map/while
  115.0 5.7 %copy-start.6 = (bf16[3072,128]{1,0:T(8,128)(2,1)}, bf16[3072,128]{1,0:T(8,128)(2,1)S(1)}, u32[]{:S(2)}) copy-start(bf16[3072,128]{1,0:T(8,128)(2,1)S(1)} %get-tuple-element.581) | copy-start | bytes 2359300 | tf_op jit(solution)/shard_map/while
  115.0 3.8 copy-start.9
  115.0 3.8 copy-start.14
  120.8 2.8 copy-start.1
  123.6 3.8 copy-start.2
  132.0 1.1 copy-start.5
  132.0 1.6 copy-start.7
  133.6 5.7 %copy-start.4 = (bf16[3072,128]{1,0:T(8,128)(2,1)}, bf16[3072,128]{1,0:T(8,128)(2,1)S(1)}, u32[]{:S(2)}) copy-start(bf16[3072,128]{1,0:T(8,128)(2,1)S(1)} %get-tuple-element.577) | copy-start | bytes 2359300 | tf_op jit(solution)/shard_map/while
  133.6 5.7 %copy-start.6 = (bf16[3072,128]{1,0:T(8,128)(2,1)}, bf16[3072,128]{1,0:T(8,128)(2,1)S(1)}, u32[]{:S(2)}) copy-start(bf16[3072,128]{1,0:T(8,128)(2,1)S(1)} %get-tuple-element.581) | copy-start | bytes 2359300 | tf_op jit(solution)/shard_map/while
  133.6 3.8 copy-start.9
  133.6 3.8 copy-start.14
  139.3 2.8 copy-start.1
  142.2 3.8 copy-start.2
  150.6 1.1 copy-start.5
  150.6 1.6 copy-start.7
  152.2 279.0 %reduce-scatter.5.cloned.1.call-start = ((), (), s32[]{:S(2)}) async-start(), calls=%async_computation.4 | async-start | bytes 17301504 | tf_op jit(solution)/shard_map/reduce_scatter | solution.py:149
  212.4 0.7 copy-start.20
  212.4 1.1 copy-start.11
  212.4 1.3 copy-start.21
  212.4 218.8 %copy-start.3 = (f32[3072,128]{1,0:T(8,128)S(1)}, f32[3072,128]{1,0:T(8,128)}, u32[]{:S(2)}) copy-start(f32[3072,128]{1,0:T(8,128)} %get-tuple-element.146) | copy-start | bytes 4718596
  212.5 300.3 %all-reduce.2.cloned.1.call-start = ((), (), s32[]{:S(2)}) async-start(), calls=%async_computation.5 | async-start | bytes 1048576 | tf_op jit(solution)/shard_map/psum | solution.py:150
  514.2 3.9 copy-start.18
  514.6 3.5 copy-start.19
Sparse Core Ops, SparseCore 0:
  152.3 49.0 reduce-scatter.2
  212.6 218.5 reduce-scatter.4
  434.0 78.6 all-reduce.1
